TPU v7x, 1024 devices: a whole 4x4x32 slice. The times are simulated.
1024 devices in a mesh: region: 128 (over z, y), local: 8 (over x, core).
Axes of the slice: x: 4, y: 4, z: 32, core: 2. Of those that a mesh axis runs over, the one named last changes fastest.
Arguments:
- atm_flux: bfloat16 [12, 4194304], P(None, ('region', 'local')), may hold values from -6 to 6
- cell_map: int32 [1024, 4096], P(('region', 'local')), may hold values from 0 to 4095, each once within a row
- neighbours: int32 [4, 4194304], P(None, ('region', 'local')), may hold values from 0 to 4095
- coef_x: float32 [4, 4194304], P(None, ('region', 'local')), may hold values from -3 to 3
- coef_y: float32 [4, 4194304], P(None, ('region', 'local')), may hold values from -3 to 3
- send_list: int32 [1024, 8, 4], P(('region', 'local')), may hold values from 0 to 31, as said below
- cover: int32 [4096, 4], P(('region', 'local')), may hold values from 0 to 31, as said below
- cover_count: int32 [4096], P(('region', 'local')), may hold values from 1 to 4
- weights: bfloat16 [4096, 4, 3, 128, 128], P(('region', 'local')), may hold values from -0.15625 to 0.15625
- ocean_map: int32 [1024, 512], P(('region', 'local')), may hold values from 0 to 511, each once within a row
Outputs:
- ocean_flux: float32 [12, 524288], P(None, ('region', 'local'))
Inputs may be any that keep to these rules, and one draw needn't show every extreme that they name: `cell_map`: each row is a permutation of one device's cells. `neighbours`: indices of coupler cells on the same device. `send_list`: each row lists 4 different source blocks of the sending device. `cover`: each row lists 4 different slots of what the owner receives from its region. `ocean_map`: each row is a permutation of one device's ocean cells.
All inputs are finite; a program needn't handle non-finite values.
Results may differ from a plain program's by a relative error of at most 0.0024.
Values may be sent and summed in bfloat16 or wider, within the bound.
A program may use at most 64 MiB of HBM per device.

v0:
```python
import jax
import jax.numpy as jnp
from jax import lax
from jax.sharding import PartitionSpec as P


def reconstruct(values, near_index, weight_x, weight_y):
    nearby = values[:, near_index]
    change = nearby - values[:, None, :]
    slope_x = jnp.sum(weight_x[None] * change, axis=1)
    slope_y = jnp.sum(weight_y[None] * change, axis=1)
    upper = jnp.maximum(values, jnp.max(nearby, axis=1))
    lower = jnp.minimum(values, jnp.min(nearby, axis=1))
    steep = jnp.abs(slope_x) + jnp.abs(slope_y)
    factor = jnp.minimum(1.0, (upper - lower) / jnp.maximum(steep, 1.0))
    return jnp.stack([values, factor * slope_x, factor * slope_y]).astype(jnp.bfloat16)


def shards(
    atm_flux,
    cell_map,
    neighbours,
    coef_x,
    coef_y,
    send_list,
    cover,
    cover_count,
    weights,
    ocean_map,
):
    fields, cells = atm_flux.shape
    region_count = lax.axis_size("region")
    local_count = lax.axis_size("local")
    piece = cells // (region_count * local_count)
    outgoing = atm_flux[:, cell_map[0]].reshape(fields, region_count, local_count, piece)
    arrived = lax.all_to_all(
        lax.all_to_all(outgoing, "region", split_axis=1, concat_axis=1, tiled=True),
        "local",
        split_axis=2,
        concat_axis=2,
        tiled=True,
    )
    coupled = arrived.reshape(fields, cells).astype(jnp.float32)
    recon = reconstruct(coupled, neighbours, coef_x, coef_y)
    block_size = weights.shape[-1]
    block_count = cells // block_size
    recon = recon.reshape(3, fields, block_count, block_size)
    pooled, lists = (
        lax.all_gather(recon, "local", axis=2, tiled=True),
        lax.all_gather(send_list, "local", axis=0, tiled=True),
    )
    member = lax.axis_index("local")
    wanted = lax.dynamic_index_in_dim(lists, member, 1, keepdims=False)
    offsets = jnp.arange(local_count, dtype=jnp.int32)[:, None] * block_count
    flat_index = (wanted + offsets).reshape(-1)
    source = pooled[:, :, flat_index]
    chosen = source[:, :, cover]
    slot_total = cover.shape[1]
    live = (jnp.arange(slot_total, dtype=jnp.int32)[None, :] < cover_count[:, None]).astype(
        jnp.bfloat16
    )
    chosen = chosen * live[None, None, :, :, None]
    remapped = jnp.einsum("bkmos,mfbks->fbo", weights, chosen, preferred_element_type=jnp.float32)
    coupler_out = remapped.reshape(fields, -1)
    ocean_cells = coupler_out.shape[1]
    leaving = coupler_out[:, ocean_map[0]].reshape(
        fields, region_count, ocean_cells // region_count
    )
    landed = lax.all_to_all(leaving, "region", split_axis=1, concat_axis=1, tiled=True)
    return landed.reshape(fields, ocean_cells)


def solution(mesh):
    return jax.shard_map(
        shards,
        mesh=mesh,
        in_specs=(
            P(None, ("region", "local")),
            P(("region", "local"), None),
            P(None, ("region", "local")),
            P(None, ("region", "local")),
            P(None, ("region", "local")),
            P(("region", "local"), None, None),
            P(("region", "local"), None),
            P(("region", "local")),
            P(("region", "local"), None, None, None, None),
            P(("region", "local"), None),
        ),
        out_specs=P(None, ("region", "local")),
        check_vma=False,
    )
```

profile of v0, /device:TPU:24, one launch (start us, length us, event | category | flops | bytes accessed | tf_op | source)
XLA Modules:
  0.0 296.8 jit_solution(6785560310268667048)
XLA Ops:
  6.5 1.5 copy.125
  8.8 15.0 %gather_fusion = bf16[4096,12]{1,0:T(8,128)(2,1)} fusion(bf16[12,4096]{0,1:T(8,128)(2,1)S(1)} %copy.125, s32[4096]{0:T(1024)S(1)} %broadcast_clamp_fusion.1), kind=kCustom, calls=%fused_computation | custom fusion | bytes 212992 | tf_op jit(solution)/shard_map/gather | solution.py:35
  23.8 1.4 copy.162
  25.2 1.9 reshape.301
  27.2 32.5 %all-to-all-start = ((bf16[128,2,192]{2,1,0:T(2,128)(2,1)}), bf16[128,2,192]{2,1,0:T(2,128)(2,1)S(1)}, u32[]{:S(2)}, u32[]{:S(2)}) async-start(bf16[128,2,192]{2,1,0:T(2,128)(2,1)} %reshape.301), calls=%async_computation | async-start | bytes 262144 | tf_op jit(solution)/shard_map/all_to_all | solution.py:37
  59.8 30.8 %all-to-all-done = bf16[128,2,192]{2,1,0:T(2,128)(2,1)S(1)} async-done(((bf16[128,2,192]{2,1,0:T(2,128)(2,1)}), bf16[128,2,192]{2,1,0:T(2,128)(2,1)S(1)}, u32[]{:S(2)}, u32[]{:S(2)}) %all-to-all-start) | async-done | bytes 98336 | tf_op jit(solution)/shard_map/all_to_all | solution.py:37
  90.6 1.3 reshape.302
  91.9 1.7 copy.127
  93.6 4.3 %all-to-all-start.1 = ((bf16[12,128,8,4]{1,3,0,2:T(4,128)(2,1)}), bf16[12,128,8,4]{1,3,0,2:T(4,128)(2,1)S(1)}, u32[]{:S(2)}, u32[]{:S(2)}) async-start(bf16[12,128,8,4]{1,3,0,2:T(4,128)(2,1)} %copy.127), calls=%async_computation.1 | async-start | bytes 196608 | tf_op jit(solution)/shard_map/all_to_all | solution.py:36
  98.0 5.7 %all-to-all-done.1 = bf16[12,128,8,4]{1,3,0,2:T(4,128)(2,1)S(1)} async-done(((bf16[12,128,8,4]{1,3,0,2:T(4,128)(2,1)}), bf16[12,128,8,4]{1,3,0,2:T(4,128)(2,1)S(1)}, u32[]{:S(2)}, u32[]{:S(2)}) %all-to-all-start.1) | async-done | bytes 98336 | tf_op jit(solution)/shard_map/all_to_all | solution.py:36
  103.7 2.9 copy.131
  106.7 56.4 %gather_fusion.1 = f32[16384,12]{1,0:T(8,128)} fusion(f32[12,4096]{0,1:T(8,128)} %bitcast.43, s32[16384]{0:T(1024)S(1)} %broadcast_clamp_fusion), kind=kCustom, calls=%fused_computation.1 | custom fusion | bytes 1638400 | tf_op jit(solution)/shard_map/gather | solution.py:8
  163.0 13.0 %fusion.13 = (f32[12,4096]{0,1:T(8,128)}, f32[12,4096]{0,1:T(8,128)}, f32[12,4096]{0,1:T(8,128)}, f32[12,4096]{0,1:T(8,128)}) fusion(f32[12,4,4096]{0,2,1:T(8,128)} %bitcast.45, f32[12,4096]{0,1:T(8,128)} %bitcast.44, f32[4,4096]{1,0:T(4,128)S(1)} %copy-done.1, f32[4,4096]{1,0:T(4,128)S(1)} %copy-done.2), kind=kLoop, calls=%fused_computation.38 | loop fusion | flops 1179648 | bytes 1900544 | tf_op jit(solution)/shard_map/reduce_max | solution.py:12
  176.1 2.2 copy.145
  178.3 2.2 copy.146
  180.5 2.2 copy.147
  182.8 2.2 copy.148
  185.1 1.0 copy.128
  187.4 11.4 %all_gather.7 = s32[8,8,4]{1,2,0:T(4,128)S(1)} all-gather(s32[1,8,4]{1,2,0:T(4,128)S(1)} %copy-done.4), channel_id=1, replica_groups=mesh['region'=128,'local'=8] {'local'}, dimensions={0}, use_global_device_ids=true | all-gather | bytes 1152 | tf_op jit(solution)/shard_map/all_gather | solution.py:50
  199.5 11.1 %all-gather.2.cloned.1.call-done = bf16[3,12,256,128]{3,2,1,0:T(8,128)(2,1)} async-done(((bf16[3,12,32,128]{3,2,1,0:T(8,128)(2,1)}), bf16[3,12,256,128]{3,2,1,0:T(8,128)(2,1)}) %all-gather.2.cloned.1.call-update) | async-done | bytes 2359312 | tf_op jit(solution)/shard_map/all_gather | solution.py:49
  210.6 4.9 %copy.137 = bf16[3,12,256,128]{3,1,2,0:T(8,128)(2,1)} copy(bf16[3,12,256,128]{3,2,1,0:T(8,128)(2,1)} %all-gather.2.cloned.1.call-done) | data formatting | bytes 4718592 | tf_op jit(solution)/shard_map/all_gather | solution.py:49
  215.5 2.5 gather_fusion.2
  219.4 1.0 gather_fusion.4
  220.4 68.7 %all_to_all.15 = f32[12,128,4]{0,2,1:T(4,128)S(1)} all-to-all(f32[12,128,4]{0,2,1:T(4,128)S(1)} %bitcast.57), channel_id=1, replica_groups=mesh['region'=128,'local'=8] {'region'}, dimensions={1} | all-to-all | bytes 49152 | tf_op jit(solution)/shard_map/all_to_all | solution.py:69
  (45 shorter events, 4.9 us)
Async XLA Ops:
  6.5 212.1 %copy-start = (bf16[4,4,3,128,128]{4,3,2,1,0:T(8,128)(2,1)S(1)}, bf16[4,4,3,128,128]{4,3,2,1,0:T(8,128)(2,1)}, u32[]{:S(2)}) copy-start(bf16[4,4,3,128,128]{4,3,2,1,0:T(8,128)(2,1)} %param.18) | copy-start | bytes 4718596
  8.8 50.9 %copy-start.3 = (s32[4,4096]{1,0:T(4,128)S(1)}, s32[4,4096]{1,0:T(4,128)}, u32[]{:S(2)}) copy-start(s32[4,4096]{1,0:T(4,128)} %param.12) | copy-start | bytes 196612
  27.2 63.4 %all-to-all-start = ((bf16[128,2,192]{2,1,0:T(2,128)(2,1)}), bf16[128,2,192]{2,1,0:T(2,128)(2,1)S(1)}, u32[]{:S(2)}, u32[]{:S(2)}) async-start(bf16[128,2,192]{2,1,0:T(2,128)(2,1)} %reshape.301), calls=%async_computation | async-start | bytes 262144 | tf_op jit(solution)/shard_map/all_to_all | solution.py:37
  93.6 10.1 %all-to-all-start.1 = ((bf16[12,128,8,4]{1,3,0,2:T(4,128)(2,1)}), bf16[12,128,8,4]{1,3,0,2:T(4,128)(2,1)S(1)}, u32[]{:S(2)}, u32[]{:S(2)}) async-start(bf16[12,128,8,4]{1,3,0,2:T(4,128)(2,1)} %copy.127), calls=%async_computation.1 | async-start | bytes 196608 | tf_op jit(solution)/shard_map/all_to_all | solution.py:36
  97.9 112.7 %all-gather.2.cloned.1.call-start = ((), (), s32[]{:S(2)}) async-start(), calls=%async_computation.3 | async-start | bytes 2654208 | tf_op jit(solution)/shard_map/all_gather | solution.py:49
  106.7 56.4 %copy-start.1 = (f32[4,4096]{1,0:T(4,128)S(1)}, f32[4,4096]{1,0:T(4,128)}, u32[]{:S(2)}) copy-start(f32[4,4096]{1,0:T(4,128)} %param.14) | copy-start | bytes 196612
  106.7 56.4 %copy-start.2 = (f32[4,4096]{1,0:T(4,128)S(1)}, f32[4,4096]{1,0:T(4,128)}, u32[]{:S(2)}) copy-start(f32[4,4096]{1,0:T(4,128)} %param.13) | copy-start | bytes 196612
  185.0 2.3 copy-start.4
  185.0 14.3 %copy-start.5 = (s32[4,4]{1,0:T(4,128)S(1)}, s32[4,4]{1,0:T(4,128)}, u32[]{:S(2)}) copy-start(s32[4,4]{1,0:T(4,128)} %param.16) | copy-start | bytes 196
  185.0 14.4 %copy-start.6 = (s32[1,512]{1,0:T(1,128)S(1)}, s32[1,512]{1,0:T(1,128)}, u32[]{:S(2)}) copy-start(s32[1,512]{1,0:T(1,128)} %param.19) | copy-start | bytes 6148
  185.1 14.4 %copy-start.7 = (s32[4]{0:T(128)S(1)}, s32[4]{0:T(128)}, u32[]{:S(2)}) copy-start(s32[4]{0:T(128)} %param.17) | copy-start | bytes 52
Sparse Core Ops, SparseCore 0:
  187.5 23.0 all-gather.1
where the time goes:
time: 298 us; the launch traced here: 297 us
  local copies, waits for them, and re-layouts  103 us (35%)
  blocking collectives  80.1 us (27%)
  waiting for transfers between devices  47.6 us (16%)
  starting transfers between devices  36.9 us (12%)
  other arithmetic  14.7 us (5%)
  between operations  13.7 us (5%)
    all_to_all x1, blocking collectives, shards(): lax.all_to_all(leaving, 'region', split_axis=1, concat_axis=1, tiled=True)  68.7 us
    gather x1, local copies, waits for them, and re-layouts, reconstruct(): nearby = values[:, near_index]  56.4 us
    all_to_all x1, starting transfers between devices, shards(): lax.all_to_all(outgoing, 'region', split_axis=1, concat_axis=1, tiled=True)  32.5 us
    all_to_all x1, waiting for transfers between devices, shards(): lax.all_to_all(outgoing, 'region', split_axis=1, concat_axis=1, tiled=True)  30.8 us
    gather x1, local copies, waits for them, and re-layouts, shards(): atm_flux[:, cell_map[0]].reshape(fields, region_count, local_count, piece)  15 us
    reduce_max x1, other arithmetic, reconstruct(): upper = jnp.maximum(values, jnp.max(nearby, axis=1))  13 us
    all_gather x1, blocking collectives, shards(): lax.all_gather(send_list, 'local', axis=0, tiled=True)  11.4 us
    all_gather x1, waiting for transfers between devices, shards(): lax.all_gather(recon, 'local', axis=2, tiled=True)  11.1 us
  transfers between devices with their start and end apart: 3, of which 3 were waited for; matrix products, arithmetic and copies ran while one was open for 0% of the time, Pallas kernels for 0%

commit v1 on v0

v1 whole, which is shorter than its diff:
```python
import jax
import jax.numpy as jnp
from jax import lax
from jax.experimental import pallas as pl
from jax.experimental.pallas import tpu as pltpu
from jax.sharding import PartitionSpec as P

MESH = pl.DeviceIdType.MESH
F = 12
FP = 16
Z, Y, L = 32, 4, 8
YL = Y * L
NB = 4
K = 4
CAP = 4
OBLK = 4
BS = 128
ABLK = 32
ROWS = 3 * FP
FAR_FIRST = sorted(range(1, Z), key=lambda i: -min(i, Z - i))


def pick(table, index):
    return jnp.take_along_axis(table, index, axis=1, mode="promise_in_bounds")


def spread(row):
    return jnp.broadcast_to(row, (8, BS))


def swap_blocks(parts, turned):
    lane = lax.broadcasted_iota(jnp.int32, (32, BS), 1)
    turned[...] = jnp.concatenate(parts, axis=0).T
    rows = [turned[pl.ds(g, 32, stride=4), :] for g in range(4)]
    result = []
    for i in range(len(parts)):
        index = i * 32 + (lane >> 2)
        total = pick(rows[0], index)
        for g in range(1, 4):
            total = jnp.where((lane & 3) == g, pick(rows[g], index), total)
        result.append(total)
    return result


def swap_fields(source, target, turned):
    for q in range(F // 4):
        parts = [source[pl.ds(4 * q + i, 32, stride=FP), :] for i in range(4)]
        for i, part in enumerate(swap_blocks(parts, turned.at[q])):
            target[pl.ds(4 * q + i, 32, stride=FP), :] = part


def look_up(table, ranks, rows):
    columns = []
    for row in rows:
        low = jnp.broadcast_to((row & 255).astype(jnp.float32), (16, BS)).astype(jnp.bfloat16)
        low = jnp.broadcast_to(low[None], (16, 16, BS)).reshape(256, BS)
        one, zero = jnp.ones((256, BS), jnp.bfloat16), jnp.zeros((256, BS), jnp.bfloat16)
        columns.append(jnp.where(ranks[...] == low, one, zero))
    product = jnp.dot(table[...], jnp.concatenate(columns, axis=1), preferred_element_type=jnp.float32)
    found = []
    for i, row in enumerate(rows):
        high = jnp.broadcast_to(row >> 8, (FP, BS))
        lanes = slice(i * BS, (i + 1) * BS)
        value = product[:FP, lanes]
        for h in range(1, 16):
            value = jnp.where(high == h, product[h * FP : (h + 1) * FP, lanes], value)
        found.append(value)
    return found


def kernel(
    atm_hbm,
    cell_map_hbm,
    neighbours_hbm,
    coef_x_hbm,
    coef_y_hbm,
    send_list_hbm,
    cover_hbm,
    cover_count_hbm,
    weights_hbm,
    ocean_map_hbm,
    out,
    atm,
    cell_map,
    neighbours,
    coef_x,
    coef_y,
    send_list,
    cover,
    cover_count,
    weights,
    ocean_map,
    ranks,
    pairs,
    table,
    mixed,
    turned,
    map_rows,
    recon,
    remapped,
    landed,
    turned_out,
    send_a,
    recv_a,
    send_b,
    recv_b,
    send_c,
    recv_c,
    send_d,
    recv_e,
    loaded,
    sent,
    arrived,
):
    region, member = lax.axis_index("region"), lax.axis_index("local")
    z, y = region // Y, region % Y
    yl = y * L + member

    def plane_peer(i):
        other = (yl + i) % YL
        return other, {"region": z * Y + other // L, "local": other % L}

    def column_peer(i):
        other = (z + i) % Z
        return other, {"region": other * Y + y, "local": member}

    def send(source, target, phase, device):
        pltpu.make_async_remote_copy(
            src_ref=source,
            dst_ref=target,
            send_sem=sent.at[phase],
            recv_sem=arrived.at[phase],
            device_id=device,
            device_id_type=MESH,
        ).start()

    def wait(buffer, semaphore):
        pltpu.make_async_copy(buffer, buffer, semaphore).wait()

    loads = [
        pltpu.make_async_copy(source, target, loaded.at[i])
        for i, (source, target) in enumerate(
            (
                (cell_map_hbm, cell_map),
                (atm_hbm, atm),
                (neighbours_hbm, neighbours),
                (coef_x_hbm, coef_x),
                (coef_y_hbm, coef_y),
                (send_list_hbm, send_list),
                (cover_hbm, cover),
                (cover_count_hbm, cover_count),
                (ocean_map_hbm, ocean_map),
                (weights_hbm, weights),
            )
        )
    ]
    barrier = pltpu.get_barrier_semaphore()

    for i in FAR_FIRST:
        pl.semaphore_signal(barrier, inc=1, device_id=column_peer(i)[1], device_id_type=MESH)

    @pl.loop(1, YL)
    def _(i):
        pl.semaphore_signal(barrier, inc=1, device_id=plane_peer(i)[1], device_id_type=MESH)

    for load in loads:
        load.start()

    ranks[...] = lax.broadcasted_iota(jnp.int32, (256, BS), 0).astype(jnp.float32).astype(jnp.bfloat16)
    for load in loads[:2]:
        load.wait()
    for h in range(32):
        lanes = slice(h * BS, (h + 1) * BS)
        start, parity = (h // 2) * FP, h % 2
        pairs[pl.ds(start, F), parity * BS : (parity + 1) * BS] = atm[:, lanes]
        map_rows[pl.ds(h, 1), :] = cell_map[:, lanes]
    cells = map_rows[...].astype(jnp.float32)
    map_rows[...] = swap_blocks([cells] * 4, turned.at[0])[0].astype(jnp.int32)

    @pl.loop(0, YL // 8)
    def _(n):
        for half in range(2):
            rows = [map_rows[pl.ds(n * 8 + half * 4 + i, 1), :] for i in range(4)]
            for i, found in enumerate(look_up(pairs, ranks, rows)):
                send_a[n * 8 + half * 4 + i] = found[:F].astype(jnp.bfloat16)

    pl.semaphore_wait(barrier, 2 * 31)

    @pl.loop(1, YL)
    def _(i):
        other, device = plane_peer(i)
        send(send_a.at[other], recv_a.at[yl], 0, device)

    recv_a[yl] = send_a[yl]
    for load in loads[2:]:
        load.wait()
    wait(recv_a.at[pl.ds(0, YL - 1)], arrived.at[0])

    for a in range(YL):
        mixed[pl.ds(a * FP, F), :] = recv_a[a].astype(jnp.float32)
    swap_fields(mixed, table, turned)
    for c in range(Z):
        send_b[c] = table[pl.ds(c * FP, F), :].astype(jnp.bfloat16)

    for i in FAR_FIRST:
        other, device = column_peer(i)
        send(send_b.at[other], recv_b.at[z], 1, device)

    recv_b[z] = send_b[z]
    wait(recv_b.at[pl.ds(0, Z - 1)], arrived.at[1])
    for h in range(32):
        parity = h % 2
        pairs[pl.ds((h // 2) * FP, F), parity * BS : (parity + 1) * BS] = recv_b[h]

    def reconstruct(b):
        lanes = pl.ds(pl.multiple_of(b * BS, BS), BS)
        near, along_x, along_y = neighbours[:, lanes], coef_x[:, lanes], coef_y[:, lanes]
        value = recv_b[b].astype(jnp.float32)
        nearby = [found[:F] for found in look_up(pairs, ranks, [near[j : j + 1] for j in range(NB)])]
        change = [found - value for found in nearby]
        slope_x = sum(along_x[j : j + 1] * change[j] for j in range(NB))
        slope_y = sum(along_y[j : j + 1] * change[j] for j in range(NB))
        upper, lower = value, value
        for found in nearby:
            upper, lower = jnp.maximum(upper, found), jnp.minimum(lower, found)
        steep = jnp.abs(slope_x) + jnp.abs(slope_y)
        factor = jnp.minimum(1.0, (upper - lower) / jnp.maximum(steep, 1.0))
        for m, term in enumerate((value, factor * slope_x, factor * slope_y)):
            recon[b, m * FP : m * FP + F, :] = term.astype(jnp.bfloat16)

    @pl.loop(0, 8)
    def _(n):
        for i in range(4):
            reconstruct(n * 4 + i)

    def gather_blocks(other):
        for k in range(CAP):
            send_c[other, k] = recon[send_list[0, k, other]]

    @pl.loop(1, L)
    def _(i):
        other = (member + i) % L
        gather_blocks(other)
        send(send_c.at[other], recv_c.at[pl.ds(member * CAP, CAP)], 2, {"region": region, "local": other})

    gather_blocks(member)
    for k in range(CAP):
        recv_c[member * CAP + k] = send_c[member, k]
    wait(recv_c.at[pl.ds(0, (L - 1) * CAP)], arrived.at[2])

    for o in range(OBLK):
        total = jnp.zeros((FP, BS), jnp.float32)
        for k in range(K):
            chosen = recv_c[cover[o, k]]
            part = jnp.zeros((FP, BS), jnp.float32)
            for m in range(3):
                part += lax.dot_general(
                    chosen[m * FP : (m + 1) * FP],
                    weights[(o * K + k) * 3 + m],
                    (((1,), (1,)), ((), ())),
                    preferred_element_type=jnp.float32,
                )
            live = jnp.minimum(jnp.maximum(cover_count[o] - k, 0), 1).astype(jnp.float32)
            total += part * live
        remapped[pl.ds(o * FP, FP), :] = total

    lane = lax.broadcasted_iota(jnp.int32, (8, BS), 1)
    row = lax.broadcasted_iota(jnp.int32, (8, BS), 0)
    for q in range(4):
        cells = pick(spread(ocean_map[:, q * BS : (q + 1) * BS]), row * 16 + (lane & 15))
        block, within = cells >> 7, cells & 127
        for a in range(2):
            total = jnp.zeros((8, BS), jnp.float32)
            for b in range(min(8, F - 8 * a)):
                value = jnp.zeros((8, BS), jnp.float32)
                for o in range(OBLK):
                    near = pick(spread(remapped[pl.ds(o * FP + 8 * a + b, 1), :]), within)
                    value = jnp.where(block == o, near, value)
                total = jnp.where((lane >> 4) == b, value, total)
            for s in range(8):
                send_d[q * 8 + s, :, a * BS : (a + 1) * BS] = total[s : s + 1, :]

    for i in FAR_FIRST:
        other, device = column_peer(i)
        send(send_d.at[other], recv_e.at[y, z], 3, device)

    recv_e[y, z] = send_d[z]
    wait(send_d.at[pl.ds(0, Z - 1)], arrived.at[3])

    @pl.loop(1, Y)
    def _(i):
        other = (y + i) % Y
        send(recv_e.at[y], recv_e.at[y], 4, {"region": z * Y + other, "local": member})

    wait(recv_e.at[pl.ds(0, Y - 1)], arrived.at[4])
    for s in range(Y):
        for t in range(Z):
            landed[pl.ds(s * Z + t, 1), :] = recv_e[s, t]
    for a in range(2):
        turned_out[a] = landed[:, a * BS : (a + 1) * BS].T
        rows = [turned_out[a, pl.ds(y * 4 + p, 8, stride=16), :] for p in range(4)]
        height = min(8, F - 8 * a)
        for c in range(4):
            index = ((lane >> 2) & 3) * 32 + c * 8 + (lane >> 4)
            total = pick(rows[0], index)
            for p in range(1, 4):
                total = jnp.where((lane & 3) == p, pick(rows[p], index), total)
            out[pl.ds(a * 8, height), c * BS : (c + 1) * BS] = total[:height]

    wait(send_a.at[pl.ds(0, YL - 1)], sent.at[0])
    wait(send_b.at[pl.ds(0, Z - 1)], sent.at[1])
    wait(send_c.at[pl.ds(0, L - 1)], sent.at[2])
    wait(send_d.at[pl.ds(0, Z - 1)], sent.at[3])
    wait(recv_e.at[pl.ds(0, Y - 1)], sent.at[4])


def shards(
    atm_flux,
    cell_map,
    neighbours,
    coef_x,
    coef_y,
    send_list,
    cover,
    cover_count,
    weights,
    ocean_map,
):
    vmem = pl.BlockSpec(memory_space=pltpu.VMEM)
    blocks = weights.reshape(OBLK * K * 3, BS, BS)
    f32, bf16 = jnp.float32, jnp.bfloat16
    return pl.pallas_call(
        kernel,
        out_shape=jax.ShapeDtypeStruct((F, OBLK * BS), f32),
        in_specs=[pl.BlockSpec(memory_space=pltpu.HBM)] * 10,
        out_specs=vmem,
        scratch_shapes=[
            pltpu.VMEM(atm_flux.shape, bf16),
            pltpu.VMEM(cell_map.shape, jnp.int32),
            pltpu.VMEM(neighbours.shape, jnp.int32),
            pltpu.VMEM(coef_x.shape, f32),
            pltpu.VMEM(coef_y.shape, f32),
            pltpu.SMEM((1, CAP, L), jnp.int32),
            pltpu.SMEM(cover.shape, jnp.int32),
            pltpu.SMEM(cover_count.shape, jnp.int32),
            pltpu.VMEM(blocks.shape, bf16),
            pltpu.VMEM(ocean_map.shape, jnp.int32),
            pltpu.VMEM((256, BS), bf16),
            pltpu.VMEM((16 * FP, 2 * BS), bf16),
            pltpu.VMEM((32 * FP, BS), f32),
            pltpu.VMEM((32 * FP, BS), f32),
            pltpu.VMEM((F // 4, BS, BS), f32),
            pltpu.VMEM((32, BS), jnp.int32),
            pltpu.VMEM((ABLK, ROWS, BS), bf16),
            pltpu.VMEM((OBLK * FP, BS), f32),
            pltpu.VMEM((Y * Z, 2 * BS), f32),
            pltpu.VMEM((2, BS, BS), f32),
            pltpu.VMEM((YL, F, BS), bf16),
            pltpu.VMEM((YL, F, BS), bf16),
            pltpu.VMEM((Z, F, BS), bf16),
            pltpu.VMEM((Z, F, BS), bf16),
            pltpu.VMEM((L, CAP, ROWS, BS), bf16),
            pltpu.VMEM((L * CAP, ROWS, BS), bf16),
            pltpu.VMEM((Z, 1, 2 * BS), f32),
            pltpu.VMEM((Y, Z, 1, 2 * BS), f32),
            pltpu.SemaphoreType.DMA((10,)),
            pltpu.SemaphoreType.DMA((5,)),
            pltpu.SemaphoreType.DMA((5,)),
        ],
        compiler_params=pltpu.CompilerParams(
            collective_id=0, has_side_effects=True, vmem_limit_bytes=62 * 2**20
        ),
    )(
        atm_flux,
        cell_map,
        neighbours,
        coef_x,
        coef_y,
        jnp.swapaxes(send_list, 1, 2),
        cover,
        cover_count,
        blocks,
        ocean_map,
    )


def solution(mesh):
    return jax.shard_map(
        shards,
        mesh=mesh,
        in_specs=(
            P(None, ("region", "local")),
            P(("region", "local"), None),
            P(None, ("region", "local")),
            P(None, ("region", "local")),
            P(None, ("region", "local")),
            P(("region", "local"), None, None),
            P(("region", "local"), None),
            P(("region", "local")),
            P(("region", "local"), None, None, None, None),
            P(("region", "local"), None),
        ),
        out_specs=P(None, ("region", "local")),
        check_vma=False,
    )
```

time: 298 us -> 77.9 us (0.26)
  the two profiles are of different devices: /device:TPU:24 before, /device:TPU:1 now
where the time goes in v1:
time: 77.9 us; the launch traced here: 77.7 us
  Pallas kernels  76.3 us (98%)
  local copies, waits for them, and re-layouts  1.38 us (2%)
    pallas_call x1, Pallas kernels, shards(): pl.pallas_call(kernel, out_shape=jax.ShapeDtypeStruct((F, OBLK * BS), f32...  76.3 us

profile of v1, /device:TPU:1, one launch (start us, length us, event | category | flops | bytes accessed | tf_op | source)
XLA Modules:
  0.0 77.7 jit_solution(12645110593757357315)
XLA Ops:
  0.0 76.3 %shard_map.100 = f32[12,512]{1,0:T(8,128)} custom-call(bf16[12,4096]{1,0:T(8,128)(2,1)} %atm_hbm.1, s32[1,4096]{1,0:T(1,128)} %cell_map_hbm.1, s32[4,4096]{1,0:T(4,128)} %neighbours_hbm.1, f32[4,4096]{1,0:T(4,128)} %coef_x_hbm.1, f32[4,4096]{1,0:T(4,128)} %coef_y_hbm.1, s32[1,4,8]{2,1,0:T(4,128)} %bitcast.3, s32[4,4]{1,0:T(4,128)} %cover_hbm.1, ...), custom_call_target="tpu_custom_call" | custom-call | tf_op jit(solution)/shard_map/pallas_call | solution.py:332
  76.3 1.4 %copy.12 = f32[12,512]{1,0:T(8,128)} copy(f32[12,512]{1,0:T(8,128)} %shard_map.100) | data formatting | bytes 49152

commit v2 on v1

--- a/solution.py
+++ b/solution.py
@@ -16,7 +16,6 @@
 OBLK = 4
 BS = 128
 ABLK = 32
-ROWS = 3 * FP
 FAR_FIRST = sorted(range(1, Z), key=lambda i: -min(i, Z - i))
 
 
@@ -49,23 +48,61 @@
             target[pl.ds(4 * q + i, 32, stride=FP), :] = part
 
 
-def look_up(table, ranks, rows):
+def one_hot(ranks, rows):
     columns = []
     for row in rows:
         low = jnp.broadcast_to((row & 255).astype(jnp.float32), (16, BS)).astype(jnp.bfloat16)
         low = jnp.broadcast_to(low[None], (16, 16, BS)).reshape(256, BS)
         one, zero = jnp.ones((256, BS), jnp.bfloat16), jnp.zeros((256, BS), jnp.bfloat16)
         columns.append(jnp.where(ranks[...] == low, one, zero))
-    product = jnp.dot(table[...], jnp.concatenate(columns, axis=1), preferred_element_type=jnp.float32)
-    found = []
-    for i, row in enumerate(rows):
-        high = jnp.broadcast_to(row >> 8, (FP, BS))
-        lanes = slice(i * BS, (i + 1) * BS)
-        value = product[:FP, lanes]
-        for h in range(1, 16):
-            value = jnp.where(high == h, product[h * FP : (h + 1) * FP, lanes], value)
-        found.append(value)
-    return found
+    return jnp.concatenate(columns, axis=1)
+
+
+def fill_pairs(pairs, table):
+    for parity in range(2):
+        lanes = slice(parity * BS, (parity + 1) * BS)
+        starts = [(2 * h + parity) * FP for h in range(16)]
+        for p in range(8):
+            rows = [table[pl.ds(start, 8), :] for start in starts[2 * p : 2 * p + 2]]
+            pairs[pl.ds(16 * p, 16), lanes] = jnp.concatenate(rows, axis=0).astype(jnp.bfloat16)
+        for p in range(4):
+            rows = [table[pl.ds(start + 8, 4), :] for start in starts[4 * p : 4 * p + 4]]
+            pairs[pl.ds(128 + 16 * p, 16), lanes] = jnp.concatenate(rows, axis=0).astype(jnp.bfloat16)
+
+
+def high_part(row):
+    return jnp.broadcast_to(row >> 8, (8, BS))
+
+
+def select_eight(product, high):
+    value = product[:8]
+    for h in range(1, 16):
+        value = jnp.where(high == h, product[8 * h : 8 * h + 8], value)
+    return value
+
+
+def select_four(product, high):
+    own = high - (lax.broadcasted_iota(jnp.int32, (8, BS), 0) >> 2)
+    value = jnp.zeros((8, BS), jnp.float32)
+    for p in range(8):
+        value = jnp.where(own == 2 * p, product[8 * p : 8 * p + 8], value)
+    return value[:4] + value[4:]
+
+
+def multiply(table, columns):
+    return jnp.dot(table, columns, preferred_element_type=jnp.float32)
+
+
+def gradients(value, nearby, along_x, along_y):
+    change = [found - value for found in nearby]
+    slope_x = sum(along_x[j : j + 1] * change[j] for j in range(NB))
+    slope_y = sum(along_y[j : j + 1] * change[j] for j in range(NB))
+    upper, lower = value, value
+    for found in nearby:
+        upper, lower = jnp.maximum(upper, found), jnp.minimum(lower, found)
+    steep = jnp.abs(slope_x) + jnp.abs(slope_y)
+    factor = jnp.minimum(1.0, (upper - lower) / jnp.maximum(steep, 1.0))
+    return value, factor * slope_x, factor * slope_y
 
 
 def kernel(
@@ -91,12 +128,14 @@
     weights,
     ocean_map,
     ranks,
+    columns,
     pairs,
     table,
     mixed,
     turned,
     map_rows,
-    recon,
+    recon_8,
+    recon_4,
     remapped,
     landed,
     turned_out,
@@ -106,11 +145,14 @@
     recv_b,
     send_c,
     recv_c,
+    send_f,
+    recv_f,
     send_d,
     recv_e,
     loaded,
     sent,
     arrived,
+    reach,
 ):
     region, member = lax.axis_index("region"), lax.axis_index("local")
     z, y = region // Y, region % Y
@@ -156,24 +198,38 @@
     ]
     barrier = pltpu.get_barrier_semaphore()
 
-    for i in FAR_FIRST:
+    for i in (1, Z - 1):
         pl.semaphore_signal(barrier, inc=1, device_id=column_peer(i)[1], device_id_type=MESH)
 
     @pl.loop(1, YL)
     def _(i):
         pl.semaphore_signal(barrier, inc=1, device_id=plane_peer(i)[1], device_id_type=MESH)
 
+    def tell(step):
+        for i in (2**step, Z - 2**step):
+            pl.semaphore_signal(
+                reach.at[step], inc=1, device_id=column_peer(i)[1], device_id_type=MESH
+            )
+
+    def hear(step):
+        pl.semaphore_wait(reach.at[step], 2)
+
     for load in loads:
         load.start()
+
+    pl.semaphore_wait(barrier, YL - 1 + 2)
+    tell(0)
+    hear(0)
+    tell(1)
 
     ranks[...] = lax.broadcasted_iota(jnp.int32, (256, BS), 0).astype(jnp.float32).astype(jnp.bfloat16)
     for load in loads[:2]:
         load.wait()
     for h in range(32):
         lanes = slice(h * BS, (h + 1) * BS)
-        start, parity = (h // 2) * FP, h % 2
-        pairs[pl.ds(start, F), parity * BS : (parity + 1) * BS] = atm[:, lanes]
+        table[pl.ds(h * FP, F), :] = atm[:, lanes].astype(jnp.float32)
         map_rows[pl.ds(h, 1), :] = cell_map[:, lanes]
+    fill_pairs(pairs, table)
     cells = map_rows[...].astype(jnp.float32)
     map_rows[...] = swap_blocks([cells] * 4, turned.at[0])[0].astype(jnp.int32)
 
@@ -181,10 +237,14 @@
     def _(n):
         for half in range(2):
             rows = [map_rows[pl.ds(n * 8 + half * 4 + i, 1), :] for i in range(4)]
-            for i, found in enumerate(look_up(pairs, ranks, rows)):
-                send_a[n * 8 + half * 4 + i] = found[:F].astype(jnp.bfloat16)
-
-    pl.semaphore_wait(barrier, 2 * 31)
+            product = multiply(pairs[...], one_hot(ranks, rows))
+            for i, row in enumerate(rows):
+                part, high = product[:, i * BS : (i + 1) * BS], high_part(row)
+                found = jnp.concatenate([select_eight(part[:128], high), select_four(part[128:], high)], axis=0)
+                send_a[n * 8 + half * 4 + i] = found.astype(jnp.bfloat16)
+
+    hear(1)
+    tell(2)
 
     @pl.loop(1, YL)
     def _(i):
@@ -192,6 +252,8 @@
         send(send_a.at[other], recv_a.at[yl], 0, device)
 
     recv_a[yl] = send_a[yl]
+    hear(2)
+    tell(3)
     for load in loads[2:]:
         load.wait()
     wait(recv_a.at[pl.ds(0, YL - 1)], arrived.at[0])
@@ -200,62 +262,84 @@
         mixed[pl.ds(a * FP, F), :] = recv_a[a].astype(jnp.float32)
     swap_fields(mixed, table, turned)
     for c in range(Z):
-        send_b[c] = table[pl.ds(c * FP, F), :].astype(jnp.bfloat16)
-
+        for q in range(F // 4):
+            send_b[c, q] = table[pl.ds(c * FP + 4 * q, 4), :].astype(jnp.bfloat16)
+
+    hear(3)
     for i in FAR_FIRST:
         other, device = column_peer(i)
         send(send_b.at[other], recv_b.at[z], 1, device)
 
     recv_b[z] = send_b[z]
+
+    @pl.loop(0, ABLK)
+    def _(b):
+        near = neighbours[:, pl.ds(pl.multiple_of(b * BS, BS), BS)]
+        columns[b] = one_hot(ranks, [near[j : j + 1] for j in range(NB)])
+
     wait(recv_b.at[pl.ds(0, Z - 1)], arrived.at[1])
-    for h in range(32):
-        parity = h % 2
-        pairs[pl.ds((h // 2) * FP, F), parity * BS : (parity + 1) * BS] = recv_b[h]
-
-    def reconstruct(b):
+    for h in range(Z):
+        for q in range(F // 4):
+            table[pl.ds(h * FP + 4 * q, 4), :] = recv_b[h, q].astype(jnp.float32)
+    fill_pairs(pairs, table)
+
+    def reconstruct(b, first, rows, select, recon):
         lanes = pl.ds(pl.multiple_of(b * BS, BS), BS)
         near, along_x, along_y = neighbours[:, lanes], coef_x[:, lanes], coef_y[:, lanes]
-        value = recv_b[b].astype(jnp.float32)
-        nearby = [found[:F] for found in look_up(pairs, ranks, [near[j : j + 1] for j in range(NB)])]
-        change = [found - value for found in nearby]
-        slope_x = sum(along_x[j : j + 1] * change[j] for j in range(NB))
-        slope_y = sum(along_y[j : j + 1] * change[j] for j in range(NB))
-        upper, lower = value, value
-        for found in nearby:
-            upper, lower = jnp.maximum(upper, found), jnp.minimum(lower, found)
-        steep = jnp.abs(slope_x) + jnp.abs(slope_y)
-        factor = jnp.minimum(1.0, (upper - lower) / jnp.maximum(steep, 1.0))
-        for m, term in enumerate((value, factor * slope_x, factor * slope_y)):
-            recon[b, m * FP : m * FP + F, :] = term.astype(jnp.bfloat16)
+        value = table[pl.ds(b * FP + first, rows), :]
+        product = multiply(pairs[16 * first : 16 * (first + rows), :], columns[b])
+        nearby = [
+            select(product[:, j * BS : (j + 1) * BS], high_part(near[j : j + 1])) for j in range(NB)
+        ]
+        for m, term in enumerate(gradients(value, nearby, along_x, along_y)):
+            recon[b, m] = term.astype(jnp.bfloat16)
+
+    def send_blocks(recon, outgoing, incoming, phase):
+        def gather_blocks(other):
+            for k in range(CAP):
+                outgoing[other, k] = recon[send_list[0, k, other]]
+
+        @pl.loop(1, L)
+        def _(i):
+            other = (member + i) % L
+            gather_blocks(other)
+            send(
+                outgoing.at[other],
+                incoming.at[pl.ds(member * CAP, CAP)],
+                phase,
+                {"region": region, "local": other},
+            )
+
+        gather_blocks(member)
+        for k in range(CAP):
+            incoming[member * CAP + k] = outgoing[member, k]
 
     @pl.loop(0, 8)
     def _(n):
         for i in range(4):
-            reconstruct(n * 4 + i)
-
-    def gather_blocks(other):
-        for k in range(CAP):
-            send_c[other, k] = recon[send_list[0, k, other]]
-
-    @pl.loop(1, L)
-    def _(i):
-        other = (member + i) % L
-        gather_blocks(other)
-        send(send_c.at[other], recv_c.at[pl.ds(member * CAP, CAP)], 2, {"region": region, "local": other})
-
-    gather_blocks(member)
-    for k in range(CAP):
-        recv_c[member * CAP + k] = send_c[member, k]
+            reconstruct(n * 4 + i, 0, 8, select_eight, recon_8)
+
+    send_blocks(recon_8, send_c, recv_c, 2)
+
+    @pl.loop(0, 8)
+    def _(n):
+        for i in range(4):
+            reconstruct(n * 4 + i, 8, 4, select_four, recon_4)
+
+    send_blocks(recon_4, send_f, recv_f, 5)
     wait(recv_c.at[pl.ds(0, (L - 1) * CAP)], arrived.at[2])
+    wait(recv_f.at[pl.ds(0, (L - 1) * CAP)], arrived.at[5])
 
     for o in range(OBLK):
         total = jnp.zeros((FP, BS), jnp.float32)
         for k in range(K):
-            chosen = recv_c[cover[o, k]]
+            eight, four = recv_c[cover[o, k]], recv_f[cover[o, k]]
             part = jnp.zeros((FP, BS), jnp.float32)
             for m in range(3):
+                fields = [eight[m].astype(jnp.float32), four[m].astype(jnp.float32)]
+                chosen = jnp.concatenate(fields + [jnp.zeros((4, BS), jnp.float32)], axis=0)
                 part += lax.dot_general(
-                    chosen[m * FP : (m + 1) * FP],
+                    chosen.astype(jnp.bfloat16),
                     weights[(o * K + k) * 3 + m],
                     (((1,), (1,)), ((), ())),
                     preferred_element_type=jnp.float32,
@@ -310,6 +394,7 @@
     wait(send_a.at[pl.ds(0, YL - 1)], sent.at[0])
     wait(send_b.at[pl.ds(0, Z - 1)], sent.at[1])
     wait(send_c.at[pl.ds(0, L - 1)], sent.at[2])
+    wait(send_f.at[pl.ds(0, L - 1)], sent.at[5])
     wait(send_d.at[pl.ds(0, Z - 1)], sent.at[3])
     wait(recv_e.at[pl.ds(0, Y - 1)], sent.at[4])
 
@@ -346,26 +431,31 @@
             pltpu.VMEM(blocks.shape, bf16),
             pltpu.VMEM(ocean_map.shape, jnp.int32),
             pltpu.VMEM((256, BS), bf16),
-            pltpu.VMEM((16 * FP, 2 * BS), bf16),
+            pltpu.VMEM((ABLK, 256, NB * BS), bf16),
+            pltpu.VMEM((16 * F, 2 * BS), bf16),
             pltpu.VMEM((32 * FP, BS), f32),
             pltpu.VMEM((32 * FP, BS), f32),
             pltpu.VMEM((F // 4, BS, BS), f32),
             pltpu.VMEM((32, BS), jnp.int32),
-            pltpu.VMEM((ABLK, ROWS, BS), bf16),
+            pltpu.VMEM((ABLK, 3, 8, BS), bf16),
+            pltpu.VMEM((ABLK, 3, 4, BS), bf16),
             pltpu.VMEM((OBLK * FP, BS), f32),
             pltpu.VMEM((Y * Z, 2 * BS), f32),
             pltpu.VMEM((2, BS, BS), f32),
             pltpu.VMEM((YL, F, BS), bf16),
             pltpu.VMEM((YL, F, BS), bf16),
-            pltpu.VMEM((Z, F, BS), bf16),
-            pltpu.VMEM((Z, F, BS), bf16),
-            pltpu.VMEM((L, CAP, ROWS, BS), bf16),
-            pltpu.VMEM((L * CAP, ROWS, BS), bf16),
+            pltpu.VMEM((Z, F // 4, 4, BS), bf16),
+            pltpu.VMEM((Z, F // 4, 4, BS), bf16),
+            pltpu.VMEM((L, CAP, 3, 8, BS), bf16),
+            pltpu.VMEM((L * CAP, 3, 8, BS), bf16),
+            pltpu.VMEM((L, CAP, 3, 4, BS), bf16),
+            pltpu.VMEM((L * CAP, 3, 4, BS), bf16),
             pltpu.VMEM((Z, 1, 2 * BS), f32),
             pltpu.VMEM((Y, Z, 1, 2 * BS), f32),
             pltpu.SemaphoreType.DMA((10,)),
-            pltpu.SemaphoreType.DMA((5,)),
-            pltpu.SemaphoreType.DMA((5,)),
+            pltpu.SemaphoreType.DMA((6,)),
+            pltpu.SemaphoreType.DMA((6,)),
+            pltpu.SemaphoreType.REGULAR((4,)),
         ],
         compiler_params=pltpu.CompilerParams(
             collective_id=0, has_side_effects=True, vmem_limit_bytes=62 * 2**20

time: 77.9 us -> 74.8 us (0.960)
  Pallas kernels: 76.3 us -> 73.2 us
    pallas_call x1, Pallas kernels: 76.3 us -> 73.2 us  [shards(): pl.pallas_call(kernel, out_shape=jax.ShapeDtypeStruct((F, OBLK * BS), f32...]
where the time goes in v2:
time: 74.8 us; the launch traced here: 74.6 us
  Pallas kernels  73.2 us (98%)
  local copies, waits for them, and re-layouts  1.38 us (2%)
    pallas_call x1, Pallas kernels, shards(): pl.pallas_call(kernel, out_shape=jax.ShapeDtypeStruct((F, OBLK * BS), f32...  73.2 us

profile of v2, /device:TPU:1, one launch (start us, length us, event | category | flops | bytes accessed | tf_op | source)
XLA Modules:
  0.0 74.6 jit_solution(16658921477098026918)
XLA Ops:
  0.0 73.2 %shard_map.100 = f32[12,512]{1,0:T(8,128)} custom-call(bf16[12,4096]{1,0:T(8,128)(2,1)} %atm_hbm.1, s32[1,4096]{1,0:T(1,128)} %cell_map_hbm.1, s32[4,4096]{1,0:T(4,128)} %neighbours_hbm.1, f32[4,4096]{1,0:T(4,128)} %coef_x_hbm.1, f32[4,4096]{1,0:T(4,128)} %coef_y_hbm.1, s32[1,4,8]{2,1,0:T(4,128)} %bitcast.3, s32[4,4]{1,0:T(4,128)} %cover_hbm.1, ...), custom_call_target="tpu_custom_call" | custom-call | tf_op jit(solution)/shard_map/pallas_call | solution.py:417
  73.2 1.4 %copy.12 = f32[12,512]{1,0:T(8,128)} copy(f32[12,512]{1,0:T(8,128)} %shard_map.100) | data formatting | bytes 49152

commit v3 on v2

--- a/solution.py
+++ b/solution.py
@@ -16,6 +16,7 @@
 OBLK = 4
 BS = 128
 ABLK = 32
+NEAR = Z // 4
 FAR_FIRST = sorted(range(1, Z), key=lambda i: -min(i, Z - i))
 
 
@@ -102,7 +103,7 @@
         upper, lower = jnp.maximum(upper, found), jnp.minimum(lower, found)
     steep = jnp.abs(slope_x) + jnp.abs(slope_y)
     factor = jnp.minimum(1.0, (upper - lower) / jnp.maximum(steep, 1.0))
-    return value, factor * slope_x, factor * slope_y
+    return factor * slope_x, factor * slope_y
 
 
 def kernel(
@@ -147,6 +148,8 @@
     recv_c,
     send_f,
     recv_f,
+    send_v,
+    recv_v,
     send_d,
     recv_e,
     loaded,
@@ -198,29 +201,19 @@
     ]
     barrier = pltpu.get_barrier_semaphore()
 
-    for i in (1, Z - 1):
-        pl.semaphore_signal(barrier, inc=1, device_id=column_peer(i)[1], device_id_type=MESH)
+    for i in sorted(range(1, NEAR + 1), reverse=True):
+        for j in (i, Z - i):
+            pl.semaphore_signal(barrier, inc=1, device_id=column_peer(j)[1], device_id_type=MESH)
+
+    for load in loads[:2]:
+        load.start()
 
     @pl.loop(1, YL)
     def _(i):
         pl.semaphore_signal(barrier, inc=1, device_id=plane_peer(i)[1], device_id_type=MESH)
 
-    def tell(step):
-        for i in (2**step, Z - 2**step):
-            pl.semaphore_signal(
-                reach.at[step], inc=1, device_id=column_peer(i)[1], device_id_type=MESH
-            )
-
-    def hear(step):
-        pl.semaphore_wait(reach.at[step], 2)
-
-    for load in loads:
+    for load in loads[2:]:
         load.start()
-
-    pl.semaphore_wait(barrier, YL - 1 + 2)
-    tell(0)
-    hear(0)
-    tell(1)
 
     ranks[...] = lax.broadcasted_iota(jnp.int32, (256, BS), 0).astype(jnp.float32).astype(jnp.bfloat16)
     for load in loads[:2]:
@@ -243,8 +236,10 @@
                 found = jnp.concatenate([select_eight(part[:128], high), select_four(part[128:], high)], axis=0)
                 send_a[n * 8 + half * 4 + i] = found.astype(jnp.bfloat16)
 
-    hear(1)
-    tell(2)
+    pl.semaphore_wait(barrier, YL - 1 + 2 * NEAR)
+    for j in (NEAR, Z - NEAR):
+        pl.semaphore_signal(reach, inc=1, device_id=column_peer(j)[1], device_id_type=MESH)
+
 
     @pl.loop(1, YL)
     def _(i):
@@ -252,8 +247,6 @@
         send(send_a.at[other], recv_a.at[yl], 0, device)
 
     recv_a[yl] = send_a[yl]
-    hear(2)
-    tell(3)
     for load in loads[2:]:
         load.wait()
     wait(recv_a.at[pl.ds(0, YL - 1)], arrived.at[0])
@@ -265,7 +258,7 @@
         for q in range(F // 4):
             send_b[c, q] = table[pl.ds(c * FP + 4 * q, 4), :].astype(jnp.bfloat16)
 
-    hear(3)
+    pl.semaphore_wait(reach, 2)
     for i in FAR_FIRST:
         other, device = column_peer(i)
         send(send_b.at[other], recv_b.at[z], 1, device)
@@ -278,66 +271,70 @@
         columns[b] = one_hot(ranks, [near[j : j + 1] for j in range(NB)])
 
     wait(recv_b.at[pl.ds(0, Z - 1)], arrived.at[1])
+    def send_blocks(*groups):
+        def gather_blocks(other):
+            for blocks, outgoing, _, _ in groups:
+                for k in range(CAP):
+                    outgoing[other, k] = blocks[send_list[0, k, other]]
+
+        @pl.loop(1, L)
+        def _(i):
+            other = (member + i) % L
+            gather_blocks(other)
+            for _, outgoing, incoming, phase in groups:
+                send(
+                    outgoing.at[other],
+                    incoming.at[pl.ds(member * CAP, CAP)],
+                    phase,
+                    {"region": region, "local": other},
+                )
+
+        gather_blocks(member)
+        for _, outgoing, incoming, _ in groups:
+            for k in range(CAP):
+                incoming[member * CAP + k] = outgoing[member, k]
+
+    send_blocks((recv_b, send_v, recv_v, 6))
+
     for h in range(Z):
         for q in range(F // 4):
             table[pl.ds(h * FP + 4 * q, 4), :] = recv_b[h, q].astype(jnp.float32)
     fill_pairs(pairs, table)
 
-    def reconstruct(b, first, rows, select, recon):
+    def reconstruct(b):
         lanes = pl.ds(pl.multiple_of(b * BS, BS), BS)
         near, along_x, along_y = neighbours[:, lanes], coef_x[:, lanes], coef_y[:, lanes]
-        value = table[pl.ds(b * FP + first, rows), :]
-        product = multiply(pairs[16 * first : 16 * (first + rows), :], columns[b])
-        nearby = [
-            select(product[:, j * BS : (j + 1) * BS], high_part(near[j : j + 1])) for j in range(NB)
-        ]
-        for m, term in enumerate(gradients(value, nearby, along_x, along_y)):
-            recon[b, m] = term.astype(jnp.bfloat16)
-
-    def send_blocks(recon, outgoing, incoming, phase):
-        def gather_blocks(other):
-            for k in range(CAP):
-                outgoing[other, k] = recon[send_list[0, k, other]]
-
-        @pl.loop(1, L)
-        def _(i):
-            other = (member + i) % L
-            gather_blocks(other)
-            send(
-                outgoing.at[other],
-                incoming.at[pl.ds(member * CAP, CAP)],
-                phase,
-                {"region": region, "local": other},
-            )
-
-        gather_blocks(member)
-        for k in range(CAP):
-            incoming[member * CAP + k] = outgoing[member, k]
-
-    @pl.loop(0, 8)
+        high = [high_part(near[j : j + 1]) for j in range(NB)]
+        product = multiply(pairs[...], columns[b])
+        parts = [product[:, j * BS : (j + 1) * BS] for j in range(NB)]
+        eight = [select_eight(parts[j][:128], high[j]) for j in range(NB)]
+        four = [select_four(parts[j][128:], high[j]) for j in range(NB)]
+        for nearby, first, rows, recon in ((eight, 0, 8, recon_8), (four, 8, 4, recon_4)):
+            value = table[pl.ds(b * FP + first, rows), :]
+            for m, term in enumerate(gradients(value, nearby, along_x, along_y)):
+                recon[b, m] = term.astype(jnp.bfloat16)
+
+    @pl.loop(0, 4)
     def _(n):
-        for i in range(4):
-            reconstruct(n * 4 + i, 0, 8, select_eight, recon_8)
-
-    send_blocks(recon_8, send_c, recv_c, 2)
-
-    @pl.loop(0, 8)
-    def _(n):
-        for i in range(4):
-            reconstruct(n * 4 + i, 8, 4, select_four, recon_4)
-
-    send_blocks(recon_4, send_f, recv_f, 5)
+        for i in range(8):
+            reconstruct(n * 8 + i)
+
+    send_blocks((recon_8, send_c, recv_c, 2), (recon_4, send_f, recv_f, 5))
+    wait(recv_v.at[pl.ds(0, (L - 1) * CAP)], arrived.at[6])
     wait(recv_c.at[pl.ds(0, (L - 1) * CAP)], arrived.at[2])
     wait(recv_f.at[pl.ds(0, (L - 1) * CAP)], arrived.at[5])
 
     for o in range(OBLK):
         total = jnp.zeros((FP, BS), jnp.float32)
         for k in range(K):
-            eight, four = recv_c[cover[o, k]], recv_f[cover[o, k]]
+            slot = cover[o, k]
+            values, eight, four = recv_v[slot], recv_c[slot], recv_f[slot]
+            fields = [[values[q] for q in range(F // 4)]]
+            fields += [[eight[m], four[m]] for m in range(2)]
             part = jnp.zeros((FP, BS), jnp.float32)
             for m in range(3):
-                fields = [eight[m].astype(jnp.float32), four[m].astype(jnp.float32)]
-                chosen = jnp.concatenate(fields + [jnp.zeros((4, BS), jnp.float32)], axis=0)
+                rows = [rows.astype(jnp.float32) for rows in fields[m]]
+                chosen = jnp.concatenate(rows + [jnp.zeros((FP - F, BS), jnp.float32)], axis=0)
                 part += lax.dot_general(
                     chosen.astype(jnp.bfloat16),
                     weights[(o * K + k) * 3 + m],
@@ -395,6 +392,7 @@
     wait(send_b.at[pl.ds(0, Z - 1)], sent.at[1])
     wait(send_c.at[pl.ds(0, L - 1)], sent.at[2])
     wait(send_f.at[pl.ds(0, L - 1)], sent.at[5])
+    wait(send_v.at[pl.ds(0, L - 1)], sent.at[6])
     wait(send_d.at[pl.ds(0, Z - 1)], sent.at[3])
     wait(recv_e.at[pl.ds(0, Y - 1)], sent.at[4])
 
@@ -437,8 +435,8 @@
             pltpu.VMEM((32 * FP, BS), f32),
             pltpu.VMEM((F // 4, BS, BS), f32),
             pltpu.VMEM((32, BS), jnp.int32),
-            pltpu.VMEM((ABLK, 3, 8, BS), bf16),
-            pltpu.VMEM((ABLK, 3, 4, BS), bf16),
+            pltpu.VMEM((ABLK, 2, 8, BS), bf16),
+            pltpu.VMEM((ABLK, 2, 4, BS), bf16),
             pltpu.VMEM((OBLK * FP, BS), f32),
             pltpu.VMEM((Y * Z, 2 * BS), f32),
             pltpu.VMEM((2, BS, BS), f32),
@@ -446,16 +444,18 @@
             pltpu.VMEM((YL, F, BS), bf16),
             pltpu.VMEM((Z, F // 4, 4, BS), bf16),
             pltpu.VMEM((Z, F // 4, 4, BS), bf16),
-            pltpu.VMEM((L, CAP, 3, 8, BS), bf16),
-            pltpu.VMEM((L * CAP, 3, 8, BS), bf16),
-            pltpu.VMEM((L, CAP, 3, 4, BS), bf16),
-            pltpu.VMEM((L * CAP, 3, 4, BS), bf16),
+            pltpu.VMEM((L, CAP, 2, 8, BS), bf16),
+            pltpu.VMEM((L * CAP, 2, 8, BS), bf16),
+            pltpu.VMEM((L, CAP, 2, 4, BS), bf16),
+            pltpu.VMEM((L * CAP, 2, 4, BS), bf16),
+            pltpu.VMEM((L, CAP, F // 4, 4, BS), bf16),
+            pltpu.VMEM((L * CAP, F // 4, 4, BS), bf16),
             pltpu.VMEM((Z, 1, 2 * BS), f32),
             pltpu.VMEM((Y, Z, 1, 2 * BS), f32),
             pltpu.SemaphoreType.DMA((10,)),
-            pltpu.SemaphoreType.DMA((6,)),
-            pltpu.SemaphoreType.DMA((6,)),
-            pltpu.SemaphoreType.REGULAR((4,)),
+            pltpu.SemaphoreType.DMA((7,)),
+            pltpu.SemaphoreType.DMA((7,)),
+            pltpu.SemaphoreType.REGULAR,
         ],
         compiler_params=pltpu.CompilerParams(
             collective_id=0, has_side_effects=True, vmem_limit_bytes=62 * 2**20

time: 74.8 us -> 70.2 us (0.939)
  Pallas kernels: 73.2 us -> 68.6 us
    pallas_call x1, Pallas kernels: 73.2 us -> 68.6 us  [shards(): pl.pallas_call(kernel, out_shape=jax.ShapeDtypeStruct((F, OBLK * BS), f32...]
where the time goes in v3:
time: 70.2 us; the launch traced here: 70 us
  Pallas kernels  68.6 us (98%)
  local copies, waits for them, and re-layouts  1.38 us (2%)
    pallas_call x1, Pallas kernels, shards(): pl.pallas_call(kernel, out_shape=jax.ShapeDtypeStruct((F, OBLK * BS), f32...  68.6 us

profile of v3, /device:TPU:1, one launch (start us, length us, event | category | flops | bytes accessed | tf_op | source)
XLA Modules:
  0.0 70.0 jit_solution(17078181664927479617)
XLA Ops:
  0.0 68.6 %shard_map.100 = f32[12,512]{1,0:T(8,128)} custom-call(bf16[12,4096]{1,0:T(8,128)(2,1)} %atm_hbm.1, s32[1,4096]{1,0:T(1,128)} %cell_map_hbm.1, s32[4,4096]{1,0:T(4,128)} %neighbours_hbm.1, f32[4,4096]{1,0:T(4,128)} %coef_x_hbm.1, f32[4,4096]{1,0:T(4,128)} %coef_y_hbm.1, s32[1,4,8]{2,1,0:T(4,128)} %bitcast.3, s32[4,4]{1,0:T(4,128)} %cover_hbm.1, ...), custom_call_target="tpu_custom_call" | custom-call | tf_op jit(solution)/shard_map/pallas_call | solution.py:415
  68.6 1.4 %copy.12 = f32[12,512]{1,0:T(8,128)} copy(f32[12,512]{1,0:T(8,128)} %shard_map.100) | data formatting | bytes 49152

commit v4 on v3

--- a/solution.py
+++ b/solution.py
@@ -272,15 +272,14 @@
 
     wait(recv_b.at[pl.ds(0, Z - 1)], arrived.at[1])
     def send_blocks(*groups):
-        def gather_blocks(other):
-            for blocks, outgoing, _, _ in groups:
-                for k in range(CAP):
-                    outgoing[other, k] = blocks[send_list[0, k, other]]
-
-        @pl.loop(1, L)
-        def _(i):
-            other = (member + i) % L
-            gather_blocks(other)
+        for other in range(L):
+            for k in range(CAP):
+                block = send_list[0, k, other]
+                for blocks, outgoing, _, _ in groups:
+                    outgoing[other, k] = blocks[block]
+
+        for i in range(1, L):
+            other = lax.rem(member + i, L)
             for _, outgoing, incoming, phase in groups:
                 send(
                     outgoing.at[other],
@@ -289,7 +288,6 @@
                     {"region": region, "local": other},
                 )
 
-        gather_blocks(member)
         for _, outgoing, incoming, _ in groups:
             for k in range(CAP):
                 incoming[member * CAP + k] = outgoing[member, k]
@@ -331,16 +329,17 @@
             values, eight, four = recv_v[slot], recv_c[slot], recv_f[slot]
             fields = [[values[q] for q in range(F // 4)]]
             fields += [[eight[m], four[m]] for m in range(2)]
-            part = jnp.zeros((FP, BS), jnp.float32)
-            for m in range(3):
-                rows = [rows.astype(jnp.float32) for rows in fields[m]]
-                chosen = jnp.concatenate(rows + [jnp.zeros((FP - F, BS), jnp.float32)], axis=0)
-                part += lax.dot_general(
-                    chosen.astype(jnp.bfloat16),
-                    weights[(o * K + k) * 3 + m],
-                    (((1,), (1,)), ((), ())),
-                    preferred_element_type=jnp.float32,
-                )
+            rest = [jnp.zeros((FP - F, BS), jnp.float32)]
+            chosen = [
+                jnp.concatenate([rows.astype(jnp.float32) for rows in parts] + rest, axis=0)
+                for parts in fields
+            ]
+            part = lax.dot_general(
+                jnp.concatenate(chosen, axis=1).astype(jnp.bfloat16),
+                jnp.concatenate([weights[(o * K + k) * 3 + m] for m in range(3)], axis=1),
+                (((1,), (1,)), ((), ())),
+                preferred_element_type=jnp.float32,
+            )
             live = jnp.minimum(jnp.maximum(cover_count[o] - k, 0), 1).astype(jnp.float32)
             total += part * live
         remapped[pl.ds(o * FP, FP), :] = total
@@ -368,8 +367,7 @@
     recv_e[y, z] = send_d[z]
     wait(send_d.at[pl.ds(0, Z - 1)], arrived.at[3])
 
-    @pl.loop(1, Y)
-    def _(i):
+    for i in (2, 1, 3):
         other = (y + i) % Y
         send(recv_e.at[y], recv_e.at[y], 4, {"region": z * Y + other, "local": member})
 

time: 70.2 us -> 69.6 us (level)
  no operation moved by 1% of the time
where the time goes in v4:
time: 69.6 us; the launch traced here: 69.3 us
  Pallas kernels  68 us (98%)
  local copies, waits for them, and re-layouts  1.38 us (2%)
    pallas_call x1, Pallas kernels, shards(): pl.pallas_call(kernel, out_shape=jax.ShapeDtypeStruct((F, OBLK * BS), f32...  68 us

profile of v4, /device:TPU:1, one launch (start us, length us, event | category | flops | bytes accessed | tf_op | source)
XLA Modules:
  0.0 69.3 jit_solution(4825846215099197712)
XLA Ops:
  0.0 68.0 %shard_map.100 = f32[12,512]{1,0:T(8,128)} custom-call(bf16[12,4096]{1,0:T(8,128)(2,1)} %atm_hbm.1, s32[1,4096]{1,0:T(1,128)} %cell_map_hbm.1, s32[4,4096]{1,0:T(4,128)} %neighbours_hbm.1, f32[4,4096]{1,0:T(4,128)} %coef_x_hbm.1, f32[4,4096]{1,0:T(4,128)} %coef_y_hbm.1, s32[1,4,8]{2,1,0:T(4,128)} %bitcast.3, s32[4,4]{1,0:T(4,128)} %cover_hbm.1, ...), custom_call_target="tpu_custom_call" | custom-call | tf_op jit(solution)/shard_map/pallas_call | solution.py:413
  68.0 1.4 %copy.12 = f32[12,512]{1,0:T(8,128)} copy(f32[12,512]{1,0:T(8,128)} %shard_map.100) | data formatting | bytes 49152
